TPU v7x, 128 devices: a whole 4x4x4 slice. The times are simulated.
128 devices in a mesh: dp: 16 (over z_hi, x, core), grad: 8 (over z_lo, y).
Axes of the slice: x: 4, y: 4, z: 4 (z_hi: 2, z_lo: 2; z = z_hi * 2 + z_lo), core: 2. Of those that a mesh axis runs over, the one named last changes fastest.
Arguments:
- inputs: bfloat16 [16384, 4096], P('dp'), may hold values from -6 to 6
- out_grads: bfloat16 [16384, 8192], P('dp'), may hold values from -0.046875 to 0.046875
- basis_g: bfloat16 [4, 2048, 2048], P(None, 'dp'), may hold values from -0.125 to 0.125
- basis_a: bfloat16 [2, 2048, 2048], P(None, 'dp'), may hold values from -0.125 to 0.125
- eig_g: float32 [4, 2048], replicated, may hold values from 0.3 to 3
- eig_a: float32 [2, 2048], replicated, may hold values from 0.3 to 3
Outputs:
- preconditioned: bfloat16 [2048, 8, 2048], P(None, 'grad')
All inputs are finite; a program needn't handle non-finite values.
Results may differ from a plain program's by a relative error of at most 0.024.
Values may be sent and summed in bfloat16 or wider, within the bound.
A program may use at most 128 MiB of HBM per device.

v0:
```python
import jax
import jax.numpy as jnp
from jax import lax
from jax.sharding import PartitionSpec as P

DAMPING = 0.05


def body(inputs, out_grads, basis_g, basis_a, eig_g, eig_a):
    n_data = lax.axis_size("dp")
    n_workers = lax.axis_size("grad")
    width = basis_g.shape[2]
    g_blocks = basis_g.shape[0]
    local = g_blocks * basis_a.shape[0] // n_workers
    share = width // n_data
    first = lax.axis_index("grad") * local
    side = first // g_blocks
    lead = first % g_blocks
    place = lax.axis_index("dp")
    tok_rows = inputs.shape[0]
    x_block = lax.dynamic_slice_in_dim(inputs, side * width, width, 1)
    dy_blocks = lax.dynamic_slice_in_dim(
        out_grads.reshape(tok_rows, g_blocks, width), lead, local, 1
    )
    summed = lax.psum_scatter(
        jnp.einsum("tr,tke->rke", x_block, dy_blocks, preferred_element_type=jnp.float32).astype(
            jnp.bfloat16
        ),
        "dp",
        scatter_dimension=0,
        tiled=True,
    )
    g_rows = lax.dynamic_slice_in_dim(basis_g, lead, local, 0)
    a_rows = lax.dynamic_index_in_dim(basis_a, side, 0, keepdims=False)
    full_g, full_a = (
        lax.all_gather(g_rows, "dp", axis=1, tiled=True),
        lax.all_gather(a_rows, "dp", axis=0, tiled=True),
    )
    rotated = jnp.einsum("rkc,kcm->rkm", summed, full_g, preferred_element_type=jnp.float32).astype(
        jnp.bfloat16
    )
    columns = lax.all_to_all(rotated, "dp", split_axis=2, concat_axis=0, tiled=True)
    inner = jnp.einsum("an,akm->nkm", full_a, columns, preferred_element_type=jnp.float32)
    lam_side = lax.dynamic_index_in_dim(eig_a, side, 0, keepdims=False)
    lam_out = lax.dynamic_slice(eig_g, (lead, place * share), (local, share))
    scaled = (inner / (lam_side[:, None, None] * lam_out[None, :, :] + DAMPING)).astype(
        jnp.bfloat16
    )
    back = jnp.einsum("an,nkm->akm", full_a, scaled, preferred_element_type=jnp.float32).astype(
        jnp.bfloat16
    )
    rows_back = lax.all_to_all(back, "dp", split_axis=0, concat_axis=2, tiled=True)
    finished = jnp.einsum(
        "rkm,kcm->rkc", rows_back, full_g, preferred_element_type=jnp.float32
    ).astype(jnp.bfloat16)
    return lax.all_gather(finished, "dp", axis=0, tiled=True)


def solution(mesh):
    in_specs = (P("dp", None), P("dp", None), P(None, "dp", None), P(None, "dp", None), P(), P())
    out_specs = P(None, "grad", None)
    return jax.shard_map(body, mesh=mesh, in_specs=in_specs, out_specs=out_specs, check_vma=False)
```

profile of v0, /device:TPU:1, one launch (start us, length us, event | category | flops | bytes accessed | tf_op | source)
XLA Modules:
  0.0 439.6 jit_solution(18351164095412912980)
XLA Ops:
  6.5 22.5 %copy.21 = bf16[1024,8192]{0,1:T(8,128)(2,1)} copy(bf16[1024,8192]{1,0:T(8,128)(2,1)} %param.7) | data formatting | bytes 33554432 | tf_op args[1]
  29.1 14.0 %convert_bitcast_fusion = bf16[2048,1,2048]{2,0,1:T(8,128)(2,1)} fusion(bf16[1024,4,2048]{0,2,1:T(8,128)(2,1)} %bitcast.65, s32[]{:T(128)S(6)} %select_n.29, bf16[1024,4096]{1,0:T(8,128)(2,1)} %param.6, s32[]{:T(128)S(6)} %select_n.32), kind=kOutput, calls=%fused_computation.8 | convolution fusion | flops 8594128896 | bytes 16777224 | tf_op jit(solution)/shard_map/tr,tke->rke/dot_general | solution.py:26
  43.2 0.9 constant_dynamic-slice_fusion.2
  45.4 102.6 %reduce-scatter.2.cloned.1.call-done = bf16[128,1,2048]{2,0,1:T(8,128)(2,1)} async-done(((bf16[2048,1,2048]{2,0,1:T(8,128)(2,1)}), bf16[128,1,2048]{2,0,1:T(8,128)(2,1)}) %reduce-scatter.2.cloned.1.call-update) | async-done | bytes 524304 | tf_op jit(solution)/shard_map/reduce_scatter | solution.py:25
  148.0 75.4 %all-gather.5.cloned.1.call-done = bf16[1,2048,2048]{2,1,0:T(8,128)(2,1)} async-done(((bf16[1,128,2048]{2,1,0:T(8,128)(2,1)}), bf16[1,2048,2048]{2,1,0:T(8,128)(2,1)}) %all-gather.5.cloned.1.call-update) | async-done | bytes 8388624 | tf_op jit(solution)/shard_map/all_gather | solution.py:36
  223.4 5.8 %fusion.26 = bf16[128,1,2048]{0,2,1:T(8,128)(2,1)S(1)} fusion(bf16[1,2048,2048]{2,1,0:T(8,128)(2,1)} %all-gather.5.cloned.1.call-done, bf16[128,1,2048]{2,0,1:T(8,128)(2,1)} %reduce-scatter.2.cloned.1.call-done), kind=kOutput, calls=%fused_computation.17 | convolution fusion | flops 1074003968 | bytes 9437184 | tf_op jit(solution)/shard_map/rkc,kcm->rkm/dot_general | solution.py:39
  229.3 8.1 %copy.31 = bf16[128,1,2048]{0,1,2:T(2,128)(2,1)S(1)} copy(bf16[128,1,2048]{0,2,1:T(8,128)(2,1)S(1)} %fusion.26) | data formatting | bytes 1048576 | tf_op jit(solution)/shard_map/convert_element_type | solution.py:39
  238.0 12.3 %reduce = bf16[2048,128]{1,0:T(8,128)(2,1)} reduce(bf16[2048,1,128]{2,1,0:T(2,128)(2,1)S(1)} %bitcast.67, bf16[]{:T(256)} %broadcast.7), dimensions={1}, to_apply=%bitcast.64.reduce_sub_computation | reduce | bytes 1048578
  250.2 2.0 reshape.50
  252.2 4.2 all-to-all-start
  257.5 13.5 %all-to-all-done = bf16[16,2,8192]{2,1,0:T(2,128)(2,1)} async-done(((bf16[16,2,8192]{2,1,0:T(2,128)(2,1)}), bf16[16,2,8192]{2,1,0:T(2,128)(2,1)}, u32[]{:S(2)}, u32[]{:S(2)}) %all-to-all-start) | async-done | bytes 524320 | tf_op jit(solution)/shard_map/all_to_all | solution.py:42
  271.0 2.2 reshape.51
  273.2 0.9 copy.28
  274.1 1.3 copy.24
  275.4 26.4 %all-gather.9.cloned.1.call-done = bf16[1,2048,2048]{2,1,0:T(8,128)(2,1)} async-done(((bf16[1,128,2048]{2,1,0:T(8,128)(2,1)}), bf16[1,2048,2048]{2,1,0:T(8,128)(2,1)}) %all-gather.9.cloned.1.call-update) | async-done | bytes 8388624 | tf_op jit(solution)/shard_map/all_gather | solution.py:37
  301.8 14.3 %fusion.20 = bf16[2048,1,128]{2,0,1:T(8,128)(2,1)S(1)} fusion(bf16[1,2048,2048]{2,1,0:T(8,128)(2,1)} %all-gather.9.cloned.1.call-done, bf16[2048,128]{1,0:T(8,128)(2,1)S(1)} %bitcast.70, f32[128]{0:T(128)S(1)} %dynamic-slice_bitcast_fusion, f32[2048]{0:T(1024)S(1)} %bitcast.72), kind=kOutput, calls=%fused_computation.15 | convolution fusion | flops 2148794368 | bytes 9445888 | tf_op jit(solution)/shard_map/an,nkm->akm/dot_general | solution.py:49
  316.1 1.0 reduce.1
  317.2 14.8 %all_to_all.30 = bf16[16,2,8192]{2,1,0:T(2,128)(2,1)} all-to-all(bf16[16,2,8192]{2,1,0:T(2,128)(2,1)S(1)} %reshape.52), channel_id=1, replica_groups=mesh['dp'=16,'grad'=8] {'dp'}, dimensions={0} | all-to-all | bytes 1048576 | tf_op jit(solution)/shard_map/all_to_all | solution.py:52
  332.1 2.2 reshape.53
  334.3 0.9 copy.29
  335.1 1.3 copy.26
  336.5 6.5 %fusion.23 = bf16[128,1,2048]{0,2,1:T(8,128)(2,1)} fusion(bf16[128,2048]{0,1:T(8,128)(2,1)S(1)} %bitcast.71, bf16[1,2048,2048]{2,1,0:T(8,128)(2,1)} %all-gather.5.cloned.1.call-done), kind=kOutput, calls=%fused_computation.16 | convolution fusion | flops 1074003968 | bytes 9437184 | tf_op jit(solution)/shard_map/rkm,kcm->rkc/dot_general | solution.py:53
  343.0 77.8 %all-gather.7.cloned.1.call-done = bf16[2048,1,2048]{0,2,1:T(8,128)(2,1)} async-done(((bf16[128,1,2048]{0,2,1:T(8,128)(2,1)}), bf16[2048,1,2048]{0,2,1:T(8,128)(2,1)}) %all-gather.7.cloned.1.call-update) | async-done | bytes 8388624 | tf_op jit(solution)/shard_map/all_gather | solution.py:56
  420.9 12.2 %copy.27 = bf16[2048,1,2048]{2,0,1:T(8,128)(2,1)} copy(bf16[2048,1,2048]{0,2,1:T(8,128)(2,1)} %all-gather.7.cloned.1.call-done) | data formatting | bytes 16777216 | tf_op jit(solution)/shard_map/all_gather | solution.py:56
  (19 shorter events, 3.1 us)
Async XLA Ops:
  6.5 36.7 %copy-start = (bf16[4,128,2048]{2,1,0:T(8,128)(2,1)S(1)}, bf16[4,128,2048]{2,1,0:T(8,128)(2,1)}, u32[]{:S(2)}) copy-start(bf16[4,128,2048]{2,1,0:T(8,128)(2,1)} %param.8) | copy-start | bytes 6291460
  6.5 141.5 %reduce-scatter.2.cloned.1.call-start = ((), (), s32[]{:S(2)}) async-start(), calls=%async_computation.4 | async-start | bytes 8912896 | tf_op jit(solution)/shard_map/reduce_scatter | solution.py:25
  43.1 1.4 copy-start.1
  43.1 180.3 %all-gather.5.cloned.1.call-start = ((), (), s32[]{:S(2)}) async-start(), calls=%async_computation.3 | async-start | bytes 8912896 | tf_op jit(solution)/shard_map/all_gather | solution.py:36
  44.1 257.7 %all-gather.9.cloned.1.call-start = ((), (), s32[]{:S(2)}) async-start(), calls=%async_computation.6 | async-start | bytes 8912896 | tf_op jit(solution)/shard_map/all_gather | solution.py:37
  45.4 212.1 %copy-start.2 = (f32[2,2048]{1,0:T(2,128)S(1)}, f32[2,2048]{1,0:T(2,128)}, u32[]{:S(2)}) copy-start(f32[2,2048]{1,0:T(2,128)} %param.11) | copy-start | bytes 49156
  252.2 18.8 %all-to-all-start = ((bf16[16,2,8192]{2,1,0:T(2,128)(2,1)}), bf16[16,2,8192]{2,1,0:T(2,128)(2,1)}, u32[]{:S(2)}, u32[]{:S(2)}) async-start(bf16[16,2,8192]{2,1,0:T(2,128)(2,1)} %reshape.50), calls=%async_computation.1 | async-start | bytes 1048576 | tf_op jit(solution)/shard_map/all_to_all | solution.py:42
  256.4 164.4 %all-gather.7.cloned.1.call-start = ((), (), s32[]{:S(2)}) async-start(), calls=%async_computation.5 | async-start | bytes 8912896 | tf_op jit(solution)/shard_map/all_gather | solution.py:56
Sparse Core Ops, SparseCore 0:
  43.3 104.7 reduce-scatter.1
  150.5 72.9 all-gather.4
  225.9 75.8 all-gather.8
  343.1 77.6 all-gather.6
where the time goes:
time: 441 us; the launch traced here: 440 us
  waiting for transfers between devices  296 us (67%)
  local copies, waits for them, and re-layouts  57 us (13%)
  matrix products  40.7 us (9%)
  blocking collectives  14.8 us (3%)
  other arithmetic  13.3 us (3%)
  between operations  13.2 us (3%)
  starting transfers between devices  4.75 us (1%)
    reduce_scatter x1, waiting for transfers between devices, body(): lax.psum_scatter(jnp.einsum('tr,tke->rke', x_block, dy_blocks, preferred_...  103 us
    all_gather x1, waiting for transfers between devices, body(): return lax.all_gather(finished, 'dp', axis=0, tiled=True)  77.8 us
    all_gather x1, waiting for transfers between devices, body(): lax.all_gather(g_rows, 'dp', axis=1, tiled=True)  75.4 us
    unnamed x14, local copies, waits for them, and re-layouts  31.5 us
    all_gather x1, waiting for transfers between devices, body(): lax.all_gather(a_rows, 'dp', axis=0, tiled=True)  26.4 us
    all_to_all x1, blocking collectives, body(): lax.all_to_all(back, 'dp', split_axis=0, concat_axis=2, tiled=True)  14.8 us
    dot_general x1, matrix products, body(): jnp.einsum('an,nkm->akm', full_a, scaled, preferred_element_type=jnp.floa...  14.3 us
    dot_general x1, matrix products, body(): jnp.einsum('tr,tke->rke', x_block, dy_blocks, preferred_element_type=jnp....  14 us
  transfers between devices with their start and end apart: 5, of which 5 were waited for; matrix products, arithmetic and copies ran while one was open for 8% of the time, Pallas kernels for 0%

commit v1 on v0

v1 whole, which is shorter than its diff:
```python
import functools

import jax
import jax.numpy as jnp
from jax import lax
from jax.experimental import pallas as pl
from jax.experimental.pallas import tpu as pltpu
from jax.sharding import PartitionSpec as P

DAMPING = 0.05
MESH = pl.DeviceIdType.MESH
BF, F32 = jnp.bfloat16, jnp.float32

NX, NZ, NY, NC = 4, 2, 4, 2
CH = NX * NZ
W = 2048
SH = W // (CH * NC)
HALF = W // NC
HS = SH // 2
TOK = 1024
BG_A = 5
RS_A = 768
R = 4
RC = W // R
AG_A = 304
N_SEM = 160


def nn(a, b):
    return lax.dot_general(a, b, (((1,), (0,)), ((), ())), preferred_element_type=F32)


def nt(a, b):
    return lax.dot_general(a, b, (((1,), (1,)), ((), ())), preferred_element_type=F32)


def row_of(table, k):
    rows = lax.broadcasted_iota(jnp.int32, table.shape, 0)
    return jnp.sum(jnp.where(rows == k, table, 0.0), axis=0, keepdims=True)


def kernel(x_hbm, y_hbm, bg_hbm, ba_hbm, eg_ref, ea_ref, out_hbm,
           xb, yb, bgs, tpeer, bgt, ba, ygt, vt, ra, rb, sa, sb, ra2, rb2, vtf, sct, back,
           ss, rs, ls):
    d = lax.axis_index("dp")
    g = lax.axis_index("grad")
    c = lax.rem(d, NC)
    x = lax.rem(lax.div(d, NC), NX)
    zh = lax.div(d, NC * NX)
    y = lax.rem(g, NY)
    zl = lax.div(g, NY)
    q = zh * NX + x

    def dp_of(z_, x_, c_):
        return (z_ * NX + x_) * NC + c_

    xs = [lax.rem(x + k, NX) for k in range(1, NX)]
    xf = [lax.rem(x + NX - k, NX) for k in range(1, NX)]
    to_x = [(dp_of(zh, p, c), g) for p in xs]
    to_z = (dp_of(1 - zh, x, c), g)
    to_c = (dp_of(zh, x, 1 - c), g)
    ys = [lax.rem(y + k, NY) for k in range(1, NY)]
    yf = [lax.rem(y + NY - k, NY) for k in range(1, NY)]
    to_y = [(d, zl * NY + p) for p in ys]

    sends = []
    count = [0]

    def slot():
        count[0] += 1
        return count[0] - 1

    def put(src, dst, dev):
        k = slot()
        cp = pltpu.make_async_remote_copy(src_ref=src, dst_ref=dst, send_sem=ss.at[k], recv_sem=rs.at[k],
                                          device_id=dev, device_id_type=MESH)
        cp.start()
        sends.append(cp)
        return k

    def got(k, dst):
        pltpu.make_async_remote_copy(src_ref=dst, dst_ref=dst, send_sem=ss.at[k], recv_sem=rs.at[k],
                                     device_id=to_c, device_id_type=MESH).wait_recv()

    load_bg = pltpu.make_async_copy(bg_hbm.at[y], bgs, ls.at[0])
    load_bg.start()
    x_src = x_hbm.at[:, pl.ds(pl.multiple_of(zl * W, W), W)]
    y_src = y_hbm.at[:, pl.ds(pl.multiple_of(y * W, W), W)]
    my_tok = pl.ds(pl.multiple_of(c * TOK, TOK), TOK)
    other_tok = pl.ds(pl.multiple_of((1 - c) * TOK, TOK), TOK)
    load_y = pltpu.make_async_copy(y_src, yb.at[my_tok], ls.at[1])
    load_x = pltpu.make_async_copy(x_src, xb.at[my_tok], ls.at[2])
    quarter = pl.ds(pl.multiple_of(y * (SH // NY), SH // NY), SH // NY)
    load_ba = pltpu.make_async_copy(ba_hbm.at[zl, quarter], ba.at[zh, x, c, y], ls.at[3])
    load_ba.start()

    barrier = pltpu.get_barrier_semaphore()
    partners = [*to_x, to_z, to_c, *to_y]
    for dev in partners:
        pl.semaphore_signal(barrier, inc=1, device_id=dev, device_id_type=MESH)
    pl.semaphore_wait(barrier, len(partners))

    load_bg.wait()
    my_lane = pl.ds(pl.multiple_of(q * 2 * SH + c * SH, SH), SH)
    peer_lane = pl.ds(pl.multiple_of(q * 2 * SH + (1 - c) * SH, SH), SH)

    def flip(p, _):
        mine = pl.ds(pl.multiple_of(c * HALF + p * SH, SH), SH)
        other = pl.ds(pl.multiple_of((1 - c) * HALF + p * SH, SH), SH)
        tpeer[p] = bgs[:, other].astype(F32).T.astype(BF)
        bgt[c, p, :, my_lane] = bgs[:, mine].astype(F32).T.astype(BF)
        return 0

    lax.fori_loop(0, CH, flip, 0)
    k_peer = put(tpeer, bgt.at[1 - c, :, :, my_lane], to_c)
    load_y.start()
    load_x.start()
    got(k_peer, bgt.at[c, :, :, peer_lane])

    def bg_piece(side, first, last, h, lanes):
        return bgt.at[side, first:last, pl.ds(h * HS, HS), lanes]

    def lanes_of(z_, x_):
        return pl.ds(pl.multiple_of((z_ * NX + x_) * 2 * SH, 2 * SH), 2 * SH)

    def bg_one(h):
        lane = lanes_of(zh, x)
        kb = put(bg_piece(c, BG_A, CH, h, lane), bg_piece(c, BG_A, CH, h, lane), to_z)
        ka = [put(bg_piece(c, 0, BG_A, h, lane), bg_piece(c, 0, BG_A, h, lane), dev) for dev in to_x]
        return ka, kb

    row_lanes = [pl.ds(pl.multiple_of(z_ * NX * 2 * SH, NX * 2 * SH), NX * 2 * SH) for z_ in (zh, 1 - zh)]

    def bg_two(h, ks):
        ka, kb = ks
        got(kb, bg_piece(c, BG_A, CH, h, lanes_of(1 - zh, x)))
        out = []
        for z_ in (zh, 1 - zh):
            lane = lanes_of(z_, x)
            out.append([put(bg_piece(c, BG_A, CH, h, lane), bg_piece(c, BG_A, CH, h, lane), dev) for dev in to_x])
        for n in range(NX - 1):
            got(ka[n], bg_piece(c, 0, BG_A, h, lanes_of(zh, xf[n])))
        k = put(bg_piece(c, 0, BG_A, h, row_lanes[0]), bg_piece(c, 0, BG_A, h, row_lanes[0]), to_z)
        return out, k

    def bg_done(h, ks):
        kb, ka = ks
        for z_, row in zip((zh, 1 - zh), kb):
            for n in range(NX - 1):
                got(row[n], bg_piece(c, BG_A, CH, h, lanes_of(z_, xf[n])))
        got(ka, bg_piece(c, 0, BG_A, h, row_lanes[1]))

    first0 = bg_one(0)
    k_y = put(y_src, yb.at[my_tok], to_c)
    k_x = put(x_src, xb.at[my_tok], to_c)

    load_ba.wait()

    def ba_piece(z_, x_, first, last):
        return ba.at[z_, x_, c, y, first:last]

    ka_b = put(ba_piece(zh, x, 16, 32), ba_piece(zh, x, 16, 32), to_z)
    ka_a = [put(ba_piece(zh, x, 0, 16), ba_piece(zh, x, 0, 16), dev) for dev in to_x]
    second0 = bg_two(0, first0)
    first1 = bg_one(1)
    got(ka_b, ba_piece(1 - zh, x, 16, 32))
    ka_b2 = [put(ba.at[:, x, c, y, 16:32], ba.at[:, x, c, y, 16:32], dev) for dev in to_x]
    for n in range(NX - 1):
        got(ka_a[n], ba_piece(zh, xf[n], 0, 16))
    ka_a2 = put(ba.at[zh, :, c, y, 0:16], ba.at[zh, :, c, y, 0:16], to_z)
    second1 = bg_two(1, first1)
    for n in range(NX - 1):
        got(ka_b2[n], ba.at[:, xf[n], c, y, 16:32])
    got(ka_a2, ba.at[1 - zh, :, c, y, 0:16])
    ka_y = [put(ba.at[:, :, c, y], ba.at[:, :, c, y], dev) for dev in to_y]

    load_y.wait()
    load_x.wait()
    got(k_y, yb.at[other_tok])
    got(k_x, xb.at[other_tok])

    def grad(h):
        def rotate(t, _):
            rows = pl.ds(pl.multiple_of(t * 256, 256), 256)
            left = bgt[c, :, pl.ds(h * HS, HS), :].reshape(CH * HS, W)
            ygt[:, rows] = nt(left, yb[rows, :]).astype(BF)
            return 0

        lax.fori_loop(0, NC * TOK // 256, rotate, 0)

        def project(t, _):
            cols = pl.ds(pl.multiple_of(t * 256, 256), 256)
            vt[h, :, :, :, cols] = nn(ygt[...], xb[:, cols]).astype(BF).reshape(NZ, NX, HS, 256)
            return 0

        lax.fori_loop(0, W // 256, project, 0)

    A, B = pl.ds(0, RS_A), pl.ds(RS_A, W - RS_A)

    def rs_one(h):
        kb = put(vt.at[h, 1 - zh, :, :, B], rb.at[h], to_z)
        ka = [put(vt.at[h, :, p, :, A], ra.at[h, n], dev) for n, (p, dev) in enumerate(zip(xs, to_x))]
        return ka, kb

    def rs_two(h, ks):
        ka, kb = ks
        got(kb, rb.at[h])
        sb[h] = (vt[h, zh, :, :, B].astype(F32) + rb[h].astype(F32)).astype(BF)
        kb2 = [put(sb.at[h, p], rb2.at[h, n], dev) for n, (p, dev) in enumerate(zip(xs, to_x))]
        for n in range(NX - 1):
            got(ka[n], ra.at[h, n])

        def total(z_):
            t = vt[h, z_, x, :, A].astype(F32)
            for n in range(NX - 1):
                t = t + ra[h, n, z_].astype(F32)
            return t

        sa[h] = total(1 - zh).astype(BF)
        ka2 = put(sa.at[h], ra2.at[h], to_z)
        vtf[pl.ds(h * HS, HS), A] = total(zh)
        return ka2, kb2

    def rs_done(h, ks):
        ka2, kb2 = ks
        rows = pl.ds(h * HS, HS)
        t = sb[h, x].astype(F32)
        for n in range(NX - 1):
            got(kb2[n], rb2.at[h, n])
            t = t + rb2[h, n].astype(F32)
        vtf[rows, B] = t
        got(ka2, ra2.at[h])
        vtf[rows, A] = vtf[rows, A] + ra2[h].astype(F32)

    bg_done(0, second0)
    grad(0)
    r0 = rs_one(0)
    bg_done(1, second1)
    k_bg = put(bgt.at[c], bgt.at[c], to_c)
    grad(1)
    r1 = rs_one(1)
    for n in range(NY - 1):
        got(ka_y[n], ba.at[:, :, c, yf[n]])
    k_ba = put(ba.at[:, :, c], ba.at[:, :, c], to_c)
    r0 = rs_two(0, r0)
    r1 = rs_two(1, r1)
    got(k_ba, ba.at[:, :, 1 - c])
    rs_done(0, r0)
    rs_done(1, r1)

    own = vtf[...].astype(BF)
    my_m = pl.ds(pl.multiple_of(c * HALF + q * SH, SH), SH)
    lam_g = jnp.broadcast_to(row_of(eg_ref[:, my_m], y), (SH, SH)).T[:, 0:1]
    vtb = sct
    vtb[0] = own

    def scale(t, _):
        cols = pl.ds(pl.multiple_of(t * 256, 256), 256)
        inner = nn(vtb[0], ba[:, :, :, :, :, cols].reshape(W, 256))
        lam = row_of(ea_ref[:, cols], zl)
        vtb[1, :, cols] = (inner / (lam_g * lam + DAMPING)).astype(BF)
        return 0

    lax.fori_loop(0, W // 256, scale, 0)

    def back_rows(r):
        left = ba[r * NZ // R, pl.ds((r * CH // R) % NX, CH // R)].reshape(RC, W)
        back[c, zh, x, pl.ds(r * RC, RC), :] = nt(left, vtb[1]).astype(BF)

    def ag_rows(r):
        return pl.ds(r * RC, AG_A), pl.ds(r * RC + AG_A, RC - AG_A)

    def ag_one(r):
        ra_, rb_ = ag_rows(r)
        kb = put(back.at[c, zh, x, rb_], back.at[c, zh, x, rb_], to_z)
        ka = [put(back.at[c, zh, x, ra_], back.at[c, zh, x, ra_], dev) for dev in to_x]
        return ka, kb

    def ag_two(r, ks):
        ka, kb = ks
        ra_, rb_ = ag_rows(r)
        got(kb, back.at[c, 1 - zh, x, rb_])
        kb2 = [put(back.at[c, :, x, rb_], back.at[c, :, x, rb_], dev) for dev in to_x]
        for n in range(NX - 1):
            got(ka[n], back.at[c, zh, xf[n], ra_])
        ka2 = put(back.at[c, zh, :, ra_], back.at[c, zh, :, ra_], to_z)
        return ka2, kb2

    def ag_core(r, ks):
        ka2, kb2 = ks
        ra_, rb_ = ag_rows(r)
        got(ka2, back.at[c, 1 - zh, :, ra_])
        for n in range(NX - 1):
            got(kb2[n], back.at[c, :, xf[n], rb_])
        rows = pl.ds(r * RC, RC)
        return put(back.at[c, :, :, rows], back.at[c, :, :, rows], to_c)

    outs = []

    def finish(r, k):
        rows = pl.ds(r * RC, RC)
        got(k, back.at[1 - c, :, :, rows])

        def block(t, _):
            cols = pl.ds(pl.multiple_of(t * 256, 256), 256)
            left = jnp.concatenate([back[k // CH, (k // NX) % NZ, k % NX, rows, :] for k in range(NC * CH)], axis=1)
            right = bgt[:, :, :, cols].reshape(W, 256)
            xb[rows, cols] = nn(left, right).astype(BF)
            return 0

        lax.fori_loop(0, W // 256, block, 0)
        cp = pltpu.make_async_copy(xb.at[rows], out_hbm.at[rows], ls.at[8 + r])
        cp.start()
        outs.append(cp)

    k1, k2, k3 = {}, {}, {}
    for r in range(R):
        back_rows(r)
        if r < 2:
            k1[r] = ag_one(r)
    got(k_bg, bgt.at[1 - c])
    for r in range(R):
        k2[r] = ag_two(r, k1[r])
        if r + 2 < R:
            k1[r + 2] = ag_one(r + 2)
        if r >= 1:
            k3[r - 1] = ag_core(r - 1, k2[r - 1])
        if r >= 2:
            finish(r - 2, k3[r - 2])
    k3[R - 1] = ag_core(R - 1, k2[R - 1])
    for r in range(R - 2, R):
        finish(r, k3[r])
    for cp in outs:
        cp.wait()
    for cp in sends:
        cp.wait_send()


def body(inputs, out_grads, basis_g, basis_a, eig_g, eig_a):
    out = pl.pallas_call(
        kernel,
        out_shape=jax.ShapeDtypeStruct((W, W), BF),
        in_specs=[pl.BlockSpec(memory_space=pl.ANY)] * 4 + [pl.BlockSpec(memory_space=pltpu.VMEM)] * 2,
        out_specs=pl.BlockSpec(memory_space=pl.ANY),
        scratch_shapes=[
            pltpu.VMEM((NC * TOK, W), BF),
            pltpu.VMEM((NC * TOK, W), BF),
            pltpu.VMEM((SH, W), BF),
            pltpu.VMEM((CH, SH, SH), BF),
            pltpu.VMEM((NC, CH, SH, W), BF),
            pltpu.VMEM((NZ, NX, NC, NY, SH // NY, W), BF),
            pltpu.VMEM((CH * HS, NC * TOK), BF),
            pltpu.VMEM((2, NZ, NX, HS, W), BF),
            pltpu.VMEM((2, NX - 1, NZ, HS, RS_A), BF),
            pltpu.VMEM((2, NX, HS, W - RS_A), BF),
            pltpu.VMEM((2, HS, RS_A), BF),
            pltpu.VMEM((2, NX, HS, W - RS_A), BF),
            pltpu.VMEM((2, HS, RS_A), BF),
            pltpu.VMEM((2, NX - 1, HS, W - RS_A), BF),
            pltpu.VMEM((SH, W), F32),
            pltpu.VMEM((2, SH, W), BF),
            pltpu.VMEM((NC, NZ, NX, W, SH), BF),
            pltpu.SemaphoreType.DMA((N_SEM,)),
            pltpu.SemaphoreType.DMA((N_SEM,)),
            pltpu.SemaphoreType.DMA((8 + R,)),
        ],
        compiler_params=pltpu.CompilerParams(collective_id=0, has_side_effects=True, vmem_limit_bytes=60 * 2**20),
        cost_estimate=pl.CostEstimate(flops=2 * W * W * W * 3, bytes_accessed=40 * 2**20, transcendentals=0),
        name="precondition",
    )(inputs, out_grads, basis_g, basis_a, eig_g, eig_a)
    return out.reshape(W, 1, W)


def solution(mesh):
    in_specs = (P("dp", None), P("dp", None), P(None, "dp", None), P(None, "dp", None), P(), P())
    out_specs = P(None, "grad", None)
    return jax.shard_map(body, mesh=mesh, in_specs=in_specs, out_specs=out_specs, check_vma=False)
```

time: 441 us -> 173 us (0.39)
  waiting for transfers between devices: 296 us -> 0 us
  Pallas kernels: 0 us -> 162 us
  local copies, waits for them, and re-layouts: 57 us -> 8.44 us
  matrix products: 40.7 us -> 0 us
  blocking collectives: 14.8 us -> 0 us
  other arithmetic: 13.3 us -> 0 us
  between operations: 13.2 us -> 0.01 us
  starting transfers between devices: 4.75 us -> 0 us
    all_gather x3 -> x0, waiting for transfers between devices: 180 us -> none  [the longest x1 77.8 us: body(): return lax.all_gather(finished, 'dp', axis=0, tiled=True)]
    pallas_call x0 -> x1, Pallas kernels: none -> 162 us  [body(): pl.pallas_call(kernel, out_shape=jax.ShapeDtypeStruct((W, W), BF), in_spe...]
    reduce_scatter x1 -> x0, waiting for transfers between devices: 103 us -> none  [body(): lax.psum_scatter(jnp.einsum('tr,tke->rke', x_block, dy_blocks, preferred_...]
    dot_general x4 -> x0, matrix products: 40.7 us -> none  [the longest x1 14.3 us: body(): jnp.einsum('an,nkm->akm', full_a, scaled, preferred_element_type=jnp.floa...]
    unnamed x14 -> x1, local copies, waits for them, and re-layouts: 31.5 us -> 8.44 us
    all_to_all x1 -> x0, blocking collectives: 14.8 us -> none  [body(): lax.all_to_all(back, 'dp', split_axis=0, concat_axis=2, tiled=True)]
    all_to_all x1 -> x0, waiting for transfers between devices: 13.5 us -> none  [body(): lax.all_to_all(rotated, 'dp', split_axis=2, concat_axis=0, tiled=True)]
    unnamed x1 -> x0, other arithmetic: 12.3 us -> none
  transfers between devices with their start and end apart: 5 -> 0, of which waited for: 5 -> 0; matrix products, arithmetic and copies ran while one was open for 8% -> 0% of each run, Pallas kernels for 0% -> 0%
where the time goes in v1:
time: 173 us; the launch traced here: 171 us
  Pallas kernels  162 us (94%)
  local copies, waits for them, and re-layouts  8.44 us (5%)
    pallas_call x1, Pallas kernels, body(): pl.pallas_call(kernel, out_shape=jax.ShapeDtypeStruct((W, W), BF), in_spe...  162 us
    unnamed x1, local copies, waits for them, and re-layouts  8.44 us

profile of v1, /device:TPU:1, one launch (start us, length us, event | category | flops | bytes accessed | tf_op | source)
XLA Modules:
  0.0 170.8 jit_solution(15840358330401704529)
XLA Ops:
  0.0 162.3 %precondition.1 = bf16[2048,2048]{1,0:T(8,128)(2,1)} custom-call(bf16[1024,4096]{1,0:T(8,128)(2,1)} %x_hbm.1, bf16[1024,8192]{1,0:T(8,128)(2,1)} %y_hbm.1, bf16[4,128,2048]{2,1,0:T(8,128)(2,1)} %bg_hbm.1, bf16[2,128,2048]{2,1,0:T(8,128)(2,1)} %ba_hbm.1, f32[4,2048]{1,0:T(4,128)} %eg_ref.1, f32[2,2048]{1,0:T(2,128)} %ea_ref.1), custom_call_target="tpu_custom_call" | custom-call | flops 51539607552 | bytes 41943040 | tf_op jit(solution)/shard_map/precondition/pallas_call | solution.py:340
  162.4 8.4 %copy.8 = bf16[2048,1,2048]{2,0,1:T(8,128)(2,1)} copy(bf16[2048,1,2048]{2,0,1:T(8,128)(2,1)} %bitcast.1) | data formatting | bytes 16777216

commit v2 on v1

v2 whole, which is shorter than its diff:
```python
import functools

import jax
import jax.numpy as jnp
from jax import lax
from jax.experimental import pallas as pl
from jax.experimental.pallas import tpu as pltpu
from jax.sharding import PartitionSpec as P

DAMPING = 0.05
MESH = pl.DeviceIdType.MESH
BF, F32 = jnp.bfloat16, jnp.float32

NX, NZ, NY, NC = 4, 2, 4, 2
CH = NX * NZ
W = 2048
SH = W // (CH * NC)
HALF = W // NC
HS = SH // 2
TOK = 1024
BG_A = 4
RS_A = 768
R = 4
RC = W // R
AG_A = 224
N_SEM = 160


def nn(a, b):
    return lax.dot_general(a, b, (((1,), (0,)), ((), ())), preferred_element_type=F32)


def nt(a, b):
    return lax.dot_general(a, b, (((1,), (1,)), ((), ())), preferred_element_type=F32)


def row_of(table, k):
    rows = lax.broadcasted_iota(jnp.int32, table.shape, 0)
    return jnp.sum(jnp.where(rows == k, table, 0.0), axis=0, keepdims=True)


def kernel(x_hbm, y_hbm, bg_hbm, ba_hbm, eg_ref, ea_ref, out_hbm,
           xb, yb, bgs, tpeer, bgt, ba, ygt, vt, rz, rbd, rod, rbf, rof, rzb, vtf, sct, back,
           ss, rs, ls):
    d = lax.axis_index("dp")
    g = lax.axis_index("grad")
    c = lax.rem(d, NC)
    x = lax.rem(lax.div(d, NC), NX)
    zh = lax.div(d, NC * NX)
    y = lax.rem(g, NY)
    zl = lax.div(g, NY)
    q = zh * NX + x

    def dp_of(z_, x_, c_):
        return (z_ * NX + x_) * NC + c_

    xp, xm, x2 = lax.rem(x + 1, NX), lax.rem(x + NX - 1, NX), lax.rem(x + 2, NX)
    to_xp, to_xm = (dp_of(zh, xp, c), g), (dp_of(zh, xm, c), g)
    to_z = (dp_of(1 - zh, x, c), g)
    to_c = (dp_of(zh, x, 1 - c), g)
    yp, ym, y2 = lax.rem(y + 1, NY), lax.rem(y + NY - 1, NY), lax.rem(y + 2, NY)
    to_yp, to_ym = (d, zl * NY + yp), (d, zl * NY + ym)

    sends = []
    count = [0]

    def slot():
        count[0] += 1
        return count[0] - 1

    def put(src, dst, dev):
        k = slot()
        cp = pltpu.make_async_remote_copy(src_ref=src, dst_ref=dst, send_sem=ss.at[k], recv_sem=rs.at[k],
                                          device_id=dev, device_id_type=MESH)
        cp.start()
        sends.append(cp)
        return k

    def got(k, dst):
        pltpu.make_async_remote_copy(src_ref=dst, dst_ref=dst, send_sem=ss.at[k], recv_sem=rs.at[k],
                                     device_id=to_c, device_id_type=MESH).wait_recv()

    load_bg = pltpu.make_async_copy(bg_hbm.at[y], bgs, ls.at[0])
    load_bg.start()
    x_src = x_hbm.at[:, pl.ds(pl.multiple_of(zl * W, W), W)]
    y_src = y_hbm.at[:, pl.ds(pl.multiple_of(y * W, W), W)]
    my_tok = pl.ds(pl.multiple_of(c * TOK, TOK), TOK)
    other_tok = pl.ds(pl.multiple_of((1 - c) * TOK, TOK), TOK)
    load_y = pltpu.make_async_copy(y_src, yb.at[my_tok], ls.at[1])
    load_x = pltpu.make_async_copy(x_src, xb.at[my_tok], ls.at[2])
    quarter = pl.ds(pl.multiple_of(y * (SH // NY), SH // NY), SH // NY)
    load_ba = pltpu.make_async_copy(ba_hbm.at[zl, quarter], ba.at[zh, x, c, y], ls.at[3])
    load_ba.start()

    barrier = pltpu.get_barrier_semaphore()
    partners = [to_xp, to_xm, to_z, to_c, to_yp, to_ym]
    for dev in partners:
        pl.semaphore_signal(barrier, inc=1, device_id=dev, device_id_type=MESH)
    pl.semaphore_wait(barrier, len(partners))

    class Gather:
        def __init__(self, ref, n, a, m, mb):
            self.ref, self.n, self.a, self.m, self.mb = ref, n, a, m, mb

        def move(self, z_, x_, first, last, dev):
            return put(self.ref(z_, x_, first, last), self.ref(z_, x_, first, last), dev)

        def one(self):
            self.p = self.move(zh, x, 0, self.n, to_xp)
            self.q = self.move(zh, x, 0, self.n, to_xm)
            self.z = self.move(zh, x, 0, self.n, to_z)

        def two(self):
            n, a, m = self.n, self.a, self.m
            got(self.p, self.ref(zh, xm, 0, n))
            self.p2 = self.move(zh, xm, 0, m, to_xp)
            self.zp = self.move(zh, xm, 0, a, to_z)
            got(self.q, self.ref(zh, xp, 0, n))
            self.q2 = self.move(zh, xp, m, n, to_xm)
            self.zq = self.move(zh, xp, 0, a, to_z)
            got(self.z, self.ref(1 - zh, x, 0, n))
            self.pb = self.move(1 - zh, x, a, n, to_xp)
            self.qb = self.move(1 - zh, x, a, n, to_xm)

        def three(self):
            n, a, m, mb = self.n, self.a, self.m, self.mb
            got(self.p2, self.ref(zh, x2, 0, m))
            self.z2 = self.move(zh, x2, 0, a, to_z)
            got(self.pb, self.ref(1 - zh, xm, a, n))
            self.pb2 = self.move(1 - zh, xm, a, mb, to_xp)
            got(self.qb, self.ref(1 - zh, xp, a, n))
            self.qb2 = self.move(1 - zh, xp, mb, n, to_xm)

        def done(self):
            n, a, m, mb = self.n, self.a, self.m, self.mb
            got(self.q2, self.ref(zh, x2, m, n))
            got(self.zp, self.ref(1 - zh, xm, 0, a))
            got(self.zq, self.ref(1 - zh, xp, 0, a))
            got(self.z2, self.ref(1 - zh, x2, 0, a))
            got(self.pb2, self.ref(1 - zh, x2, a, mb))
            got(self.qb2, self.ref(1 - zh, x2, mb, n))

    load_ba.wait()
    ga = Gather(lambda z_, x_, first, last: ba.at[z_, x_, c, y, :, first:last], W, W // 2, W // 2, 3 * W // 4)
    ga.one()

    load_bg.wait()
    my_lane = pl.ds(pl.multiple_of(q * 2 * SH + c * SH, SH), SH)
    peer_lane = pl.ds(pl.multiple_of(q * 2 * SH + (1 - c) * SH, SH), SH)

    def flip(p, _):
        mine = pl.ds(pl.multiple_of(c * HALF + p * SH, SH), SH)
        other = pl.ds(pl.multiple_of((1 - c) * HALF + p * SH, SH), SH)
        tpeer[p] = bgs[:, other].astype(F32).T.astype(BF)
        bgt[c, p, :, my_lane] = bgs[:, mine].astype(F32).T.astype(BF)
        return 0

    lax.fori_loop(0, CH, flip, 0)
    k_peer = put(tpeer, bgt.at[1 - c, :, :, my_lane], to_c)
    load_y.start()
    load_x.start()
    got(k_peer, bgt.at[c, :, :, peer_lane])

    def bg_ref(h):
        def ref(z_, x_, first, last):
            lanes = pl.ds(pl.multiple_of((z_ * NX + x_) * 2 * SH, 2 * SH), 2 * SH)
            return bgt.at[c, first:last, pl.ds(h * HS, HS), lanes]

        return ref

    gb = [Gather(bg_ref(h), CH, BG_A, CH // 2, (CH + BG_A) // 2) for h in range(2)]
    gb[0].one()
    k_y = put(y_src, yb.at[my_tok], to_c)
    k_x = put(x_src, xb.at[my_tok], to_c)

    def grad(h, first, last):
        def rotate(t, _):
            rows = pl.ds(pl.multiple_of(t * 256, 256), 256)
            left = bgt[c, :, pl.ds(h * HS, HS), :].reshape(CH * HS, W)
            ygt[:, rows] = nt(left, yb[rows, :]).astype(BF)
            return 0

        lax.fori_loop(first, last, rotate, 0)

    def outer(h, first, last):
        def project(t, _):
            cols = pl.ds(pl.multiple_of(t * 256, 256), 256)
            vt[h, :, :, :, cols] = nn(ygt[...], xb[:, cols]).astype(BF).reshape(NZ, NX, HS, 256)
            return 0

        lax.fori_loop(first, last, project, 0)

    A, B = pl.ds(0, RS_A), pl.ds(RS_A, W - RS_A)
    B0, B1 = pl.ds(RS_A, (W - RS_A) // 2), pl.ds((W + RS_A) // 2, (W - RS_A) // 2)
    H0, H1 = pl.ds(0, W // 2), pl.ds(W // 2, W // 2)

    def plus(a, b):
        return (a.astype(F32) + b.astype(F32)).astype(BF)

    class Scatter:
        def __init__(self, h):
            self.h = h

        def one(self):
            h, o = self.h, 1 - zh
            self.z2 = put(vt.at[h, o, x2, :, A], rz.at[h, 0], to_z)
            self.bd0 = put(vt.at[h, o, x2, :, B0], rbd.at[h, 0], to_xp)
            self.bd1 = put(vt.at[h, o, x2, :, B1], rbd.at[h, 1], to_xm)
            self.od1 = put(vt.at[h, zh, x2, :, H1], rod.at[h, 1], to_xm)
            self.zp = put(vt.at[h, o, xp, :, A], rz.at[h, 1], to_z)
            self.zq = put(vt.at[h, o, xm, :, A], rz.at[h, 2], to_z)
            self.zo = put(vt.at[h, o, x, :, A], rz.at[h, 3], to_z)

        def two(self):
            h, o = self.h, 1 - zh
            got(self.z2, rz.at[h, 0])
            vt[h, zh, x2, :, A] = plus(vt[h, zh, x2, :, A], rz[h, 0])
            self.od0 = put(vt.at[h, zh, x2, :, H0], rod.at[h, 0], to_xp)
            got(self.bd0, rbd.at[h, 0])
            vt[h, o, xp, :, B0] = plus(vt[h, o, xp, :, B0], rbd[h, 0])
            self.bf0 = put(vt.at[h, o, xp, :, B], rbf.at[h, 0], to_xp)
            got(self.bd1, rbd.at[h, 1])
            vt[h, o, xm, :, B1] = plus(vt[h, o, xm, :, B1], rbd[h, 1])
            self.bf1 = put(vt.at[h, o, xm, :, B], rbf.at[h, 1], to_xm)

        def three(self):
            h, o = self.h, 1 - zh
            got(self.zq, rz.at[h, 2])
            vt[h, zh, xm, :, A] = plus(vt[h, zh, xm, :, A], rz[h, 2])
            got(self.od1, rod.at[h, 1])
            vt[h, zh, xm, :, H1] = plus(vt[h, zh, xm, :, H1], rod[h, 1])
            self.of1 = put(vt.at[h, zh, xm], rof.at[h, 1], to_xm)
            got(self.zp, rz.at[h, 1])
            vt[h, zh, xp, :, A] = plus(vt[h, zh, xp, :, A], rz[h, 1])
            got(self.od0, rod.at[h, 0])
            vt[h, zh, xp, :, H0] = plus(vt[h, zh, xp, :, H0], rod[h, 0])
            self.of0 = put(vt.at[h, zh, xp], rof.at[h, 0], to_xp)
            got(self.bf0, rbf.at[h, 0])
            got(self.bf1, rbf.at[h, 1])
            t = vt[h, o, x, :, B].astype(F32) + rbf[h, 0].astype(F32) + rbf[h, 1].astype(F32)
            vt[h, o, x, :, B] = t.astype(BF)
            self.zb = put(vt.at[h, o, x, :, B], rzb.at[h], to_z)

        def done(self):
            h = self.h
            got(self.zo, rz.at[h, 3])
            got(self.of0, rof.at[h, 0])
            got(self.of1, rof.at[h, 1])
            got(self.zb, rzb.at[h])
            t = vt[h, zh, x].astype(F32) + rof[h, 0].astype(F32) + rof[h, 1].astype(F32)
            rows = pl.ds(h * HS, HS)
            vtf[rows, A] = t[:, :RS_A] + rz[h, 3].astype(F32)
            vtf[rows, B] = t[:, RS_A:] + rzb[h].astype(F32)

    sc = [Scatter(h) for h in range(2)]

    def ba_part(y_):
        return ba.at[:, :, c, y_]

    def ba_theirs(y_):
        return ba.at[:, :, 1 - c, y_]

    ga.two()
    gb[0].two()
    ga.three()
    gb[1].one()
    ga.done()
    k_yp = put(ba_part(y), ba_part(y), to_yp)
    k_ym = put(ba_part(y), ba_part(y), to_ym)
    gb[0].three()
    gb[1].two()
    load_y.wait()
    load_x.wait()
    got(k_y, yb.at[other_tok])
    got(k_x, xb.at[other_tok])
    k_c = [put(ba_part(y), ba_part(y), to_c)]
    gb[0].done()
    grad(0, 0, 4)
    gb[1].three()
    grad(0, 4, 8)
    outer(0, 0, 8)
    sc[0].one()
    gb[1].done()
    k_bg = put(bgt.at[c], bgt.at[c], to_c)
    got(k_yp, ba_part(ym))
    k_yp2 = put(ba.at[0, :, c, ym], ba.at[0, :, c, ym], to_yp)
    got(k_ym, ba_part(yp))
    k_ym2 = put(ba.at[1, :, c, yp], ba.at[1, :, c, yp], to_ym)
    k_c += [put(ba_part(ym), ba_part(ym), to_c), put(ba_part(yp), ba_part(yp), to_c)]
    grad(1, 0, 8)
    sc[0].two()
    outer(1, 0, 4)
    sc[0].three()
    outer(1, 4, 8)
    sc[1].one()
    got(k_yp2, ba.at[0, :, c, y2])
    got(k_ym2, ba.at[1, :, c, y2])
    k_c.append(put(ba_part(y2), ba_part(y2), to_c))
    sc[1].two()
    sc[0].done()
    sc[1].three()
    for k, y_ in zip(k_c, (y, ym, yp, y2)):
        got(k, ba_theirs(y_))
    sc[1].done()

    own = vtf[...].astype(BF)
    my_m = pl.ds(pl.multiple_of(c * HALF + q * SH, SH), SH)
    lam_g = jnp.broadcast_to(row_of(eg_ref[:, my_m], y), (SH, SH)).T[:, 0:1]
    vtb = sct
    vtb[0] = own

    def scale(t, _):
        cols = pl.ds(pl.multiple_of(t * 256, 256), 256)
        inner = nn(vtb[0], ba[:, :, :, :, :, cols].reshape(W, 256))
        lam = row_of(ea_ref[:, cols], zl)
        vtb[1, :, cols] = (inner / (lam_g * lam + DAMPING)).astype(BF)
        return 0

    lax.fori_loop(0, W // 256, scale, 0)

    def back_rows(r):
        left = ba[r * NZ // R, pl.ds((r * CH // R) % NX, CH // R)].reshape(RC, W)
        back[c, zh, x, pl.ds(r * RC, RC), :] = nt(left, vtb[1]).astype(BF)

    def back_ref(r):
        return lambda z_, x_, first, last: back.at[c, z_, x_, pl.ds(r * RC + first, last - first)]

    gr = [Gather(back_ref(r), RC, AG_A, RC // 2, (RC + AG_A) // 2) for r in range(R)]

    def to_core(r):
        rows = pl.ds(r * RC, RC)
        return put(back.at[c, :, :, rows], back.at[c, :, :, rows], to_c)

    outs = []

    def finish(r, k):
        rows = pl.ds(r * RC, RC)
        got(k, back.at[1 - c, :, :, rows])

        def block(t, _):
            cols = pl.ds(pl.multiple_of(t * 256, 256), 256)
            left = jnp.concatenate([back[k // CH, (k // NX) % NZ, k % NX, rows, :] for k in range(NC * CH)], axis=1)
            right = bgt[:, :, :, cols].reshape(W, 256)
            xb[rows, cols] = nn(left, right).astype(BF)
            return 0

        lax.fori_loop(0, W // 256, block, 0)
        cp = pltpu.make_async_copy(xb.at[rows], out_hbm.at[rows], ls.at[8 + r])
        cp.start()
        outs.append(cp)

    k3 = {}
    for r in range(R):
        back_rows(r)
        if r < 2:
            gr[r].one()
    got(k_bg, bgt.at[1 - c])
    for r in range(R + 3):
        if r < R:
            gr[r].two()
        if 1 <= r <= R:
            gr[r - 1].three()
        if r + 2 < R:
            gr[r + 2].one()
        if 2 <= r <= R + 1:
            gr[r - 2].done()
            k3[r - 2] = to_core(r - 2)
        if r >= 3:
            finish(r - 3, k3[r - 3])
    for cp in outs:
        cp.wait()
    for cp in sends:
        cp.wait_send()


def body(inputs, out_grads, basis_g, basis_a, eig_g, eig_a):
    out = pl.pallas_call(
        kernel,
        out_shape=jax.ShapeDtypeStruct((W, W), BF),
        in_specs=[pl.BlockSpec(memory_space=pl.ANY)] * 4 + [pl.BlockSpec(memory_space=pltpu.VMEM)] * 2,
        out_specs=pl.BlockSpec(memory_space=pl.ANY),
        scratch_shapes=[
            pltpu.VMEM((NC * TOK, W), BF),
            pltpu.VMEM((NC * TOK, W), BF),
            pltpu.VMEM((SH, W), BF),
            pltpu.VMEM((CH, SH, SH), BF),
            pltpu.VMEM((NC, CH, SH, W), BF),
            pltpu.VMEM((NZ, NX, NC, NY, SH // NY, W), BF),
            pltpu.VMEM((CH * HS, NC * TOK), BF),
            pltpu.VMEM((2, NZ, NX, HS, W), BF),
            pltpu.VMEM((2, NX, HS, RS_A), BF),
            pltpu.VMEM((2, 2, HS, (W - RS_A) // 2), BF),
            pltpu.VMEM((2, 2, HS, W // 2), BF),
            pltpu.VMEM((2, 2, HS, W - RS_A), BF),
            pltpu.VMEM((2, 2, HS, W), BF),
            pltpu.VMEM((2, HS, W - RS_A), BF),
            pltpu.VMEM((SH, W), F32),
            pltpu.VMEM((2, SH, W), BF),
            pltpu.VMEM((NC, NZ, NX, W, SH), BF),
            pltpu.SemaphoreType.DMA((N_SEM,)),
            pltpu.SemaphoreType.DMA((N_SEM,)),
            pltpu.SemaphoreType.DMA((8 + R,)),
        ],
        compiler_params=pltpu.CompilerParams(collective_id=0, has_side_effects=True, vmem_limit_bytes=60 * 2**20),
        cost_estimate=pl.CostEstimate(flops=2 * W * W * W * 3, bytes_accessed=40 * 2**20, transcendentals=0),
        name="precondition",
    )(inputs, out_grads, basis_g, basis_a, eig_g, eig_a)
    return out.reshape(W, 1, W)


def solution(mesh):
    in_specs = (P("dp", None), P("dp", None), P(None, "dp", None), P(None, "dp", None), P(), P())
    out_specs = P(None, "grad", None)
    return jax.shard_map(body, mesh=mesh, in_specs=in_specs, out_specs=out_specs, check_vma=False)
```

time: 173 us -> 153 us (0.88)
  Pallas kernels: 162 us -> 144 us
    pallas_call x1, Pallas kernels: 162 us -> 144 us  [body(): pl.pallas_call(kernel, out_shape=jax.ShapeDtypeStruct((W, W), BF), in_spe...]
where the time goes in v2:
time: 153 us; the launch traced here: 152 us
  Pallas kernels  144 us (94%)
  local copies, waits for them, and re-layouts  8.44 us (6%)
    pallas_call x1, Pallas kernels, body(): pl.pallas_call(kernel, out_shape=jax.ShapeDtypeStruct((W, W), BF), in_spe...  144 us
    unnamed x1, local copies, waits for them, and re-layouts  8.44 us

profile of v2, /device:TPU:1, one launch (start us, length us, event | category | flops | bytes accessed | tf_op | source)
XLA Modules:
  0.0 152.0 jit_solution(4290231133602886380)
XLA Ops:
  0.0 143.6 %precondition.1 = bf16[2048,2048]{1,0:T(8,128)(2,1)} custom-call(bf16[1024,4096]{1,0:T(8,128)(2,1)} %x_hbm.1, bf16[1024,8192]{1,0:T(8,128)(2,1)} %y_hbm.1, bf16[4,128,2048]{2,1,0:T(8,128)(2,1)} %bg_hbm.1, bf16[2,128,2048]{2,1,0:T(8,128)(2,1)} %ba_hbm.1, f32[4,2048]{1,0:T(4,128)} %eg_ref.1, f32[2,2048]{1,0:T(2,128)} %ea_ref.1), custom_call_target="tpu_custom_call" | custom-call | flops 51539607552 | bytes 41943040 | tf_op jit(solution)/shard_map/precondition/pallas_call | solution.py:377
  143.6 8.4 %copy.8 = bf16[2048,1,2048]{2,0,1:T(8,128)(2,1)} copy(bf16[2048,1,2048]{2,0,1:T(8,128)(2,1)} %bitcast.1) | data formatting | bytes 16777216

commit v3 on v2

--- a/solution.py
+++ b/solution.py
@@ -20,10 +20,13 @@
 TOK = 1024
 BG_A = 4
 RS_A = 768
-R = 4
-RC = W // R
-AG_A = 224
+WIDE = 512
+SIZE = (512, 512, 512, 256, 256)
+R = len(SIZE)
+ROWS = tuple(sum(SIZE[:r]) for r in range(R))
+LAST_Z = tuple(n * 7 // 16 // 32 * 32 for n in SIZE)
 N_SEM = 160
+PARTS = 8
 
 
 def nn(a, b):
@@ -39,8 +42,8 @@
     return jnp.sum(jnp.where(rows == k, table, 0.0), axis=0, keepdims=True)
 
 
-def kernel(x_hbm, y_hbm, bg_hbm, ba_hbm, eg_ref, ea_ref, out_hbm,
-           xb, yb, bgs, tpeer, bgt, ba, ygt, vt, rz, rbd, rod, rbf, rof, rzb, vtf, sct, back,
+def kernel(x_hbm, y_hbm, bg_hbm, ba_hbm, eg_ref, ea_ref, xb,
+           yb, bgs, tpeer, bgt, ba, ygt, vt, rz, rbd, rod, rbf, rof, rzb, vtf, sct, back,
            ss, rs, ls):
     d = lax.axis_index("dp")
     g = lax.axis_index("grad")
@@ -151,8 +154,8 @@
     def flip(p, _):
         mine = pl.ds(pl.multiple_of(c * HALF + p * SH, SH), SH)
         other = pl.ds(pl.multiple_of((1 - c) * HALF + p * SH, SH), SH)
-        tpeer[p] = bgs[:, other].astype(F32).T.astype(BF)
-        bgt[c, p, :, my_lane] = bgs[:, mine].astype(F32).T.astype(BF)
+        tpeer[p] = bgs[:, other].T
+        bgt[c, p, :, my_lane] = bgs[:, mine].T
         return 0
 
     lax.fori_loop(0, CH, flip, 0)
@@ -175,7 +178,7 @@
 
     def grad(h, first, last):
         def rotate(t, _):
-            rows = pl.ds(pl.multiple_of(t * 256, 256), 256)
+            rows = pl.ds(pl.multiple_of(t * WIDE, WIDE), WIDE)
             left = bgt[c, :, pl.ds(h * HS, HS), :].reshape(CH * HS, W)
             ygt[:, rows] = nt(left, yb[rows, :]).astype(BF)
             return 0
@@ -184,8 +187,8 @@
 
     def outer(h, first, last):
         def project(t, _):
-            cols = pl.ds(pl.multiple_of(t * 256, 256), 256)
-            vt[h, :, :, :, cols] = nn(ygt[...], xb[:, cols]).astype(BF).reshape(NZ, NX, HS, 256)
+            cols = pl.ds(pl.multiple_of(t * WIDE, WIDE), WIDE)
+            vt[h, :, :, :, cols] = nn(ygt[...], xb[:, cols]).astype(BF).reshape(NZ, NX, HS, WIDE)
             return 0
 
         lax.fori_loop(first, last, project, 0)
@@ -275,10 +278,10 @@
     got(k_x, xb.at[other_tok])
     k_c = [put(ba_part(y), ba_part(y), to_c)]
     gb[0].done()
-    grad(0, 0, 4)
+    grad(0, 0, 2)
     gb[1].three()
-    grad(0, 4, 8)
-    outer(0, 0, 8)
+    grad(0, 2, 4)
+    outer(0, 0, 4)
     sc[0].one()
     gb[1].done()
     k_bg = put(bgt.at[c], bgt.at[c], to_c)
@@ -287,11 +290,11 @@
     got(k_ym, ba_part(yp))
     k_ym2 = put(ba.at[1, :, c, yp], ba.at[1, :, c, yp], to_ym)
     k_c += [put(ba_part(ym), ba_part(ym), to_c), put(ba_part(yp), ba_part(yp), to_c)]
-    grad(1, 0, 8)
+    grad(1, 0, 4)
     sc[0].two()
-    outer(1, 0, 4)
+    outer(1, 0, 2)
     sc[0].three()
-    outer(1, 4, 8)
+    outer(1, 2, 4)
     sc[1].one()
     got(k_yp2, ba.at[0, :, c, y2])
     got(k_ym2, ba.at[1, :, c, y2])
@@ -310,44 +313,38 @@
     vtb[0] = own
 
     def scale(t, _):
-        cols = pl.ds(pl.multiple_of(t * 256, 256), 256)
-        inner = nn(vtb[0], ba[:, :, :, :, :, cols].reshape(W, 256))
+        cols = pl.ds(pl.multiple_of(t * WIDE, WIDE), WIDE)
+        inner = nn(vtb[0], ba[:, :, :, :, :, cols].reshape(W, WIDE))
         lam = row_of(ea_ref[:, cols], zl)
         vtb[1, :, cols] = (inner / (lam_g * lam + DAMPING)).astype(BF)
         return 0
 
-    lax.fori_loop(0, W // 256, scale, 0)
+    lax.fori_loop(0, W // WIDE, scale, 0)
 
     def back_rows(r):
-        left = ba[r * NZ // R, pl.ds((r * CH // R) % NX, CH // R)].reshape(RC, W)
-        back[c, zh, x, pl.ds(r * RC, RC), :] = nt(left, vtb[1]).astype(BF)
+        left = ba.reshape(W, W)[pl.ds(ROWS[r], SIZE[r]), :]
+        back[c, zh, x, pl.ds(ROWS[r], SIZE[r]), :] = nt(left, vtb[1]).astype(BF)
 
     def back_ref(r):
-        return lambda z_, x_, first, last: back.at[c, z_, x_, pl.ds(r * RC + first, last - first)]
-
-    gr = [Gather(back_ref(r), RC, AG_A, RC // 2, (RC + AG_A) // 2) for r in range(R)]
+        return lambda z_, x_, first, last: back.at[c, z_, x_, pl.ds(ROWS[r] + first, last - first)]
+
+    gr = [Gather(back_ref(r), SIZE[r], LAST_Z[r], SIZE[r] // 2, (SIZE[r] + LAST_Z[r]) // 2) for r in range(R)]
 
     def to_core(r):
-        rows = pl.ds(r * RC, RC)
+        rows = pl.ds(ROWS[r], SIZE[r])
         return put(back.at[c, :, :, rows], back.at[c, :, :, rows], to_c)
 
-    outs = []
-
-    def finish(r, k):
-        rows = pl.ds(r * RC, RC)
-        got(k, back.at[1 - c, :, :, rows])
+    def finish(r, part):
+        rows = pl.ds(ROWS[r], SIZE[r])
 
         def block(t, _):
-            cols = pl.ds(pl.multiple_of(t * 256, 256), 256)
+            cols = pl.ds(pl.multiple_of(t * WIDE, WIDE), WIDE)
             left = jnp.concatenate([back[k // CH, (k // NX) % NZ, k % NX, rows, :] for k in range(NC * CH)], axis=1)
-            right = bgt[:, :, :, cols].reshape(W, 256)
-            xb[rows, cols] = nn(left, right).astype(BF)
+            xb[rows, cols] = nn(left, bgt[:, :, :, cols].reshape(W, WIDE)).astype(BF)
             return 0
 
-        lax.fori_loop(0, W // 256, block, 0)
-        cp = pltpu.make_async_copy(xb.at[rows], out_hbm.at[rows], ls.at[8 + r])
-        cp.start()
-        outs.append(cp)
+        half = W // 2
+        lax.fori_loop(part * half // WIDE, (part + 1) * half // WIDE, block, 0)
 
     k3 = {}
     for r in range(R):
@@ -358,29 +355,39 @@
     for r in range(R + 3):
         if r < R:
             gr[r].two()
+        if r + 2 < R:
+            gr[r + 2].one()
+        if r >= 3:
+            got(k3[r - 3], back.at[1 - c, :, :, pl.ds(ROWS[r - 3], SIZE[r - 3])])
+            finish(r - 3, 0)
         if 1 <= r <= R:
             gr[r - 1].three()
-        if r + 2 < R:
-            gr[r + 2].one()
         if 2 <= r <= R + 1:
             gr[r - 2].done()
             k3[r - 2] = to_core(r - 2)
         if r >= 3:
-            finish(r - 3, k3[r - 3])
-    for cp in outs:
-        cp.wait()
+            finish(r - 3, 1)
     for cp in sends:
         cp.wait_send()
+
+
+def store(src, dst, sem):
+    copies = []
+    for k in range(PARTS):
+        rows = pl.ds(k * (W // PARTS), W // PARTS)
+        copies.append(pltpu.make_async_copy(src.at[rows], dst.at[rows], sem.at[k]))
+        copies[-1].start()
+    for cp in copies:
+        cp.wait()
 
 
 def body(inputs, out_grads, basis_g, basis_a, eig_g, eig_a):
     out = pl.pallas_call(
         kernel,
-        out_shape=jax.ShapeDtypeStruct((W, W), BF),
+        out_shape=pltpu.VMEM((W, W), BF),
         in_specs=[pl.BlockSpec(memory_space=pl.ANY)] * 4 + [pl.BlockSpec(memory_space=pltpu.VMEM)] * 2,
-        out_specs=pl.BlockSpec(memory_space=pl.ANY),
+        out_specs=pl.BlockSpec(memory_space=pltpu.VMEM),
         scratch_shapes=[
-            pltpu.VMEM((NC * TOK, W), BF),
             pltpu.VMEM((NC * TOK, W), BF),
             pltpu.VMEM((SH, W), BF),
             pltpu.VMEM((CH, SH, SH), BF),
@@ -399,12 +406,21 @@
             pltpu.VMEM((NC, NZ, NX, W, SH), BF),
             pltpu.SemaphoreType.DMA((N_SEM,)),
             pltpu.SemaphoreType.DMA((N_SEM,)),
-            pltpu.SemaphoreType.DMA((8 + R,)),
+            pltpu.SemaphoreType.DMA((4,)),
         ],
-        compiler_params=pltpu.CompilerParams(collective_id=0, has_side_effects=True, vmem_limit_bytes=60 * 2**20),
+        compiler_params=pltpu.CompilerParams(collective_id=0, has_side_effects=True, vmem_limit_bytes=51 * 2**20),
         cost_estimate=pl.CostEstimate(flops=2 * W * W * W * 3, bytes_accessed=40 * 2**20, transcendentals=0),
         name="precondition",
     )(inputs, out_grads, basis_g, basis_a, eig_g, eig_a)
+    out = pl.pallas_call(
+        store,
+        out_shape=jax.ShapeDtypeStruct((W, W), BF),
+        in_specs=[pl.BlockSpec(memory_space=pl.ANY)],
+        out_specs=pl.BlockSpec(memory_space=pl.ANY),
+        scratch_shapes=[pltpu.SemaphoreType.DMA((PARTS,))],
+        compiler_params=pltpu.CompilerParams(vmem_limit_bytes=2**20),
+        name="store",
+    )(pltpu.with_memory_space_constraint(out, pltpu.VMEM))
     return out.reshape(W, 1, W)
 
 

time: 153 us -> 140 us (0.915)
  local copies, waits for them, and re-layouts: 8.44 us -> 0 us
  Pallas kernels: 144 us -> 139 us
    unnamed x1 -> x0, local copies, waits for them, and re-layouts: 8.44 us -> none
    pallas_call x1 -> x2, Pallas kernels: 144 us -> 139 us  [the longest x1 136 us: body(): pl.pallas_call(kernel, out_shape=pltpu.VMEM((W, W), BF), in_specs=[pl.Blo...]
where the time goes in v3:
time: 140 us
  Pallas kernels  139 us (99%)
    pallas_call x1, Pallas kernels, body(): pl.pallas_call(kernel, out_shape=pltpu.VMEM((W, W), BF), in_specs=[pl.Blo...  136 us
    pallas_call x1, Pallas kernels, body(): pl.pallas_call(store, out_shape=jax.ShapeDtypeStruct((W, W), BF), in_spec...  3.37 us

profile of v3, /device:TPU:1, one launch (start us, length us, event | category | flops | bytes accessed | tf_op | source)
XLA Modules:
  0.0 139.6 jit_solution(2288402504024832105)
XLA Ops:
  0.0 136.1 %precondition.1.src = bf16[2048,2048]{1,0:T(8,128)(2,1)S(1)} custom-call(bf16[1024,4096]{1,0:T(8,128)(2,1)} %x_hbm.1, bf16[1024,8192]{1,0:T(8,128)(2,1)} %y_hbm.1, bf16[4,128,2048]{2,1,0:T(8,128)(2,1)} %bg_hbm.1, bf16[2,128,2048]{2,1,0:T(8,128)(2,1)} %ba_hbm.1, f32[4,2048]{1,0:T(4,128)} %eg_ref.1, f32[2,2048]{1,0:T(2,128)} %ea_ref.1), custom_call_target="tpu_custom_call" | custom-call | flops 51539607552 | bytes 41943040 | tf_op jit(solution)/shard_map/precondition/pallas_call | solution.py:385
  136.1 3.4 %store.1 = bf16[2048,2048]{1,0:T(8,128)(2,1)} custom-call(bf16[2048,2048]{1,0:T(8,128)(2,1)S(1)} %precondition.1.src), custom_call_target="tpu_custom_call" | custom-call | tf_op jit(solution)/shard_map/store/pallas_call | solution.py:415

commit v4 on v3

--- a/solution.py
+++ b/solution.py
@@ -16,7 +16,8 @@
 W = 2048
 SH = W // (CH * NC)
 HALF = W // NC
-HS = SH // 2
+HS = (80, 48)
+HO = (0, 80)
 TOK = 1024
 BG_A = 4
 RS_A = 768
@@ -167,7 +168,7 @@
     def bg_ref(h):
         def ref(z_, x_, first, last):
             lanes = pl.ds(pl.multiple_of((z_ * NX + x_) * 2 * SH, 2 * SH), 2 * SH)
-            return bgt.at[c, first:last, pl.ds(h * HS, HS), lanes]
+            return bgt.at[c, first:last, pl.ds(HO[h], HS[h]), lanes]
 
         return ref
 
@@ -179,8 +180,8 @@
     def grad(h, first, last):
         def rotate(t, _):
             rows = pl.ds(pl.multiple_of(t * WIDE, WIDE), WIDE)
-            left = bgt[c, :, pl.ds(h * HS, HS), :].reshape(CH * HS, W)
-            ygt[:, rows] = nt(left, yb[rows, :]).astype(BF)
+            left = bgt[c, :, pl.ds(HO[h], HS[h]), :].reshape(CH * HS[h], W)
+            ygt[pl.ds(0, CH * HS[h]), rows] = nt(left, yb[rows, :]).astype(BF)
             return 0
 
         lax.fori_loop(first, last, rotate, 0)
@@ -188,7 +189,8 @@
     def outer(h, first, last):
         def project(t, _):
             cols = pl.ds(pl.multiple_of(t * WIDE, WIDE), WIDE)
-            vt[h, :, :, :, cols] = nn(ygt[...], xb[:, cols]).astype(BF).reshape(NZ, NX, HS, WIDE)
+            prod = nn(ygt[pl.ds(0, CH * HS[h]), :], xb[:, cols]).astype(BF)
+            vt[:, :, pl.ds(HO[h], HS[h]), cols] = prod.reshape(NZ, NX, HS[h], WIDE)
             return 0
 
         lax.fori_loop(first, last, project, 0)
@@ -202,58 +204,60 @@
 
     class Scatter:
         def __init__(self, h):
-            self.h = h
-
-        def one(self):
-            h, o = self.h, 1 - zh
-            self.z2 = put(vt.at[h, o, x2, :, A], rz.at[h, 0], to_z)
-            self.bd0 = put(vt.at[h, o, x2, :, B0], rbd.at[h, 0], to_xp)
-            self.bd1 = put(vt.at[h, o, x2, :, B1], rbd.at[h, 1], to_xm)
-            self.od1 = put(vt.at[h, zh, x2, :, H1], rod.at[h, 1], to_xm)
-            self.zp = put(vt.at[h, o, xp, :, A], rz.at[h, 1], to_z)
-            self.zq = put(vt.at[h, o, xm, :, A], rz.at[h, 2], to_z)
-            self.zo = put(vt.at[h, o, x, :, A], rz.at[h, 3], to_z)
+            self.r = pl.ds(HO[h], HS[h])
+
+        def one_a(self):
+            r, o = self.r, 1 - zh
+            self.z2 = put(vt.at[o, x2, r, A], rz.at[0, r], to_z)
+            self.zp = put(vt.at[o, xp, r, A], rz.at[1, r], to_z)
+            self.zq = put(vt.at[o, xm, r, A], rz.at[2, r], to_z)
+            self.zo = put(vt.at[o, x, r, A], rz.at[3, r], to_z)
+
+        def one_b(self):
+            r, o = self.r, 1 - zh
+            self.bd0 = put(vt.at[o, x2, r, B0], rbd.at[0, r], to_xp)
+            self.bd1 = put(vt.at[o, x2, r, B1], rbd.at[1, r], to_xm)
+            self.od1 = put(vt.at[zh, x2, r, H1], rod.at[1, r], to_xm)
 
         def two(self):
-            h, o = self.h, 1 - zh
-            got(self.z2, rz.at[h, 0])
-            vt[h, zh, x2, :, A] = plus(vt[h, zh, x2, :, A], rz[h, 0])
-            self.od0 = put(vt.at[h, zh, x2, :, H0], rod.at[h, 0], to_xp)
-            got(self.bd0, rbd.at[h, 0])
-            vt[h, o, xp, :, B0] = plus(vt[h, o, xp, :, B0], rbd[h, 0])
-            self.bf0 = put(vt.at[h, o, xp, :, B], rbf.at[h, 0], to_xp)
-            got(self.bd1, rbd.at[h, 1])
-            vt[h, o, xm, :, B1] = plus(vt[h, o, xm, :, B1], rbd[h, 1])
-            self.bf1 = put(vt.at[h, o, xm, :, B], rbf.at[h, 1], to_xm)
+            r, o = self.r, 1 - zh
+            got(self.z2, rz.at[0, r])
+            vt[zh, x2, r, A] = plus(vt[zh, x2, r, A], rz[0, r])
+            self.od0 = put(vt.at[zh, x2, r, H0], rod.at[0, r], to_xp)
+            got(self.bd0, rbd.at[0, r])
+            vt[o, xp, r, B0] = plus(vt[o, xp, r, B0], rbd[0, r])
+            self.bf0 = put(vt.at[o, xp, r, B], rbf.at[0, r], to_xp)
+            got(self.bd1, rbd.at[1, r])
+            vt[o, xm, r, B1] = plus(vt[o, xm, r, B1], rbd[1, r])
+            self.bf1 = put(vt.at[o, xm, r, B], rbf.at[1, r], to_xm)
 
         def three(self):
-            h, o = self.h, 1 - zh
-            got(self.zq, rz.at[h, 2])
-            vt[h, zh, xm, :, A] = plus(vt[h, zh, xm, :, A], rz[h, 2])
-            got(self.od1, rod.at[h, 1])
-            vt[h, zh, xm, :, H1] = plus(vt[h, zh, xm, :, H1], rod[h, 1])
-            self.of1 = put(vt.at[h, zh, xm], rof.at[h, 1], to_xm)
-            got(self.zp, rz.at[h, 1])
-            vt[h, zh, xp, :, A] = plus(vt[h, zh, xp, :, A], rz[h, 1])
-            got(self.od0, rod.at[h, 0])
-            vt[h, zh, xp, :, H0] = plus(vt[h, zh, xp, :, H0], rod[h, 0])
-            self.of0 = put(vt.at[h, zh, xp], rof.at[h, 0], to_xp)
-            got(self.bf0, rbf.at[h, 0])
-            got(self.bf1, rbf.at[h, 1])
-            t = vt[h, o, x, :, B].astype(F32) + rbf[h, 0].astype(F32) + rbf[h, 1].astype(F32)
-            vt[h, o, x, :, B] = t.astype(BF)
-            self.zb = put(vt.at[h, o, x, :, B], rzb.at[h], to_z)
+            r, o = self.r, 1 - zh
+            got(self.zq, rz.at[2, r])
+            vt[zh, xm, r, A] = plus(vt[zh, xm, r, A], rz[2, r])
+            got(self.od1, rod.at[1, r])
+            vt[zh, xm, r, H1] = plus(vt[zh, xm, r, H1], rod[1, r])
+            self.of1 = put(vt.at[zh, xm, r], rof.at[1, r], to_xm)
+            got(self.zp, rz.at[1, r])
+            vt[zh, xp, r, A] = plus(vt[zh, xp, r, A], rz[1, r])
+            got(self.od0, rod.at[0, r])
+            vt[zh, xp, r, H0] = plus(vt[zh, xp, r, H0], rod[0, r])
+            self.of0 = put(vt.at[zh, xp, r], rof.at[0, r], to_xp)
+            got(self.bf0, rbf.at[0, r])
+            got(self.bf1, rbf.at[1, r])
+            t = vt[o, x, r, B].astype(F32) + rbf[0, r].astype(F32) + rbf[1, r].astype(F32)
+            vt[o, x, r, B] = t.astype(BF)
+            self.zb = put(vt.at[o, x, r, B], rzb.at[r], to_z)
 
         def done(self):
-            h = self.h
-            got(self.zo, rz.at[h, 3])
-            got(self.of0, rof.at[h, 0])
-            got(self.of1, rof.at[h, 1])
-            got(self.zb, rzb.at[h])
-            t = vt[h, zh, x].astype(F32) + rof[h, 0].astype(F32) + rof[h, 1].astype(F32)
-            rows = pl.ds(h * HS, HS)
-            vtf[rows, A] = t[:, :RS_A] + rz[h, 3].astype(F32)
-            vtf[rows, B] = t[:, RS_A:] + rzb[h].astype(F32)
+            r = self.r
+            got(self.zo, rz.at[3, r])
+            got(self.of0, rof.at[0, r])
+            got(self.of1, rof.at[1, r])
+            got(self.zb, rzb.at[r])
+            t = vt[zh, x, r].astype(F32) + rof[0, r].astype(F32) + rof[1, r].astype(F32)
+            vtf[r, A] = t[:, :RS_A] + rz[3, r].astype(F32)
+            vtf[r, B] = t[:, RS_A:] + rzb[r].astype(F32)
 
     sc = [Scatter(h) for h in range(2)]
 
@@ -281,27 +285,32 @@
     grad(0, 0, 2)
     gb[1].three()
     grad(0, 2, 4)
-    outer(0, 0, 4)
-    sc[0].one()
-    gb[1].done()
-    k_bg = put(bgt.at[c], bgt.at[c], to_c)
+    outer(0, 0, 2)
+    sc[0].one_a()
     got(k_yp, ba_part(ym))
     k_yp2 = put(ba.at[0, :, c, ym], ba.at[0, :, c, ym], to_yp)
     got(k_ym, ba_part(yp))
     k_ym2 = put(ba.at[1, :, c, yp], ba.at[1, :, c, yp], to_ym)
     k_c += [put(ba_part(ym), ba_part(ym), to_c), put(ba_part(yp), ba_part(yp), to_c)]
-    grad(1, 0, 4)
+    outer(0, 2, 4)
+    sc[0].one_b()
+    gb[1].done()
+    k_bg = put(bgt.at[c], bgt.at[c], to_c)
+    grad(1, 0, 2)
     sc[0].two()
-    outer(1, 0, 2)
+    grad(1, 2, 4)
+    outer(1, 0, 1)
     sc[0].three()
+    outer(1, 1, 2)
+    sc[1].one_a()
     outer(1, 2, 4)
-    sc[1].one()
+    sc[1].one_b()
+    sc[0].done()
+    sc[1].two()
+    sc[1].three()
     got(k_yp2, ba.at[0, :, c, y2])
     got(k_ym2, ba.at[1, :, c, y2])
     k_c.append(put(ba_part(y2), ba_part(y2), to_c))
-    sc[1].two()
-    sc[0].done()
-    sc[1].three()
     for k, y_ in zip(k_c, (y, ym, yp, y2)):
         got(k, ba_theirs(y_))
     sc[1].done()
@@ -393,14 +402,14 @@
             pltpu.VMEM((CH, SH, SH), BF),
             pltpu.VMEM((NC, CH, SH, W), BF),
             pltpu.VMEM((NZ, NX, NC, NY, SH // NY, W), BF),
-            pltpu.VMEM((CH * HS, NC * TOK), BF),
-            pltpu.VMEM((2, NZ, NX, HS, W), BF),
-            pltpu.VMEM((2, NX, HS, RS_A), BF),
-            pltpu.VMEM((2, 2, HS, (W - RS_A) // 2), BF),
-            pltpu.VMEM((2, 2, HS, W // 2), BF),
-            pltpu.VMEM((2, 2, HS, W - RS_A), BF),
-            pltpu.VMEM((2, 2, HS, W), BF),
-            pltpu.VMEM((2, HS, W - RS_A), BF),
+            pltpu.VMEM((CH * max(HS), NC * TOK), BF),
+            pltpu.VMEM((NZ, NX, SH, W), BF),
+            pltpu.VMEM((NX, SH, RS_A), BF),
+            pltpu.VMEM((2, SH, (W - RS_A) // 2), BF),
+            pltpu.VMEM((2, SH, W // 2), BF),
+            pltpu.VMEM((2, SH, W - RS_A), BF),
+            pltpu.VMEM((2, SH, W), BF),
+            pltpu.VMEM((SH, W - RS_A), BF),
             pltpu.VMEM((SH, W), F32),
             pltpu.VMEM((2, SH, W), BF),
             pltpu.VMEM((NC, NZ, NX, W, SH), BF),

time: 140 us -> 145 us (1.036)
  Pallas kernels: 139 us -> 145 us
    pallas_call x1, Pallas kernels: 136 us -> 141 us  [body(): pl.pallas_call(kernel, out_shape=pltpu.VMEM((W, W), BF), in_specs=[pl.Blo...]
where the time goes in v4:
time: 145 us
  Pallas kernels  145 us (100%)
    pallas_call x1, Pallas kernels, body(): pl.pallas_call(kernel, out_shape=pltpu.VMEM((W, W), BF), in_specs=[pl.Blo...  141 us
    pallas_call x1, Pallas kernels, body(): pl.pallas_call(store, out_shape=jax.ShapeDtypeStruct((W, W), BF), in_spec...  3.37 us

profile of v4, /device:TPU:1, one launch (start us, length us, event | category | flops | bytes accessed | tf_op | source)
XLA Modules:
  0.0 144.9 jit_solution(8649167982268369989)
XLA Ops:
  0.0 141.4 %precondition.1.src = bf16[2048,2048]{1,0:T(8,128)(2,1)S(1)} custom-call(bf16[1024,4096]{1,0:T(8,128)(2,1)} %x_hbm.1, bf16[1024,8192]{1,0:T(8,128)(2,1)} %y_hbm.1, bf16[4,128,2048]{2,1,0:T(8,128)(2,1)} %bg_hbm.1, bf16[2,128,2048]{2,1,0:T(8,128)(2,1)} %ba_hbm.1, f32[4,2048]{1,0:T(4,128)} %eg_ref.1, f32[2,2048]{1,0:T(2,128)} %ea_ref.1), custom_call_target="tpu_custom_call" | custom-call | flops 51539607552 | bytes 41943040 | tf_op jit(solution)/shard_map/precondition/pallas_call | solution.py:394
  141.4 3.4 %store.1 = bf16[2048,2048]{1,0:T(8,128)(2,1)} custom-call(bf16[2048,2048]{1,0:T(8,128)(2,1)S(1)} %precondition.1.src), custom_call_target="tpu_custom_call" | custom-call | tf_op jit(solution)/shard_map/store/pallas_call | solution.py:424
